TPU v7x, 512 devices: a whole 4x4x16 slice. The times are simulated.
512 devices in a mesh: dp: 32 (over z, core), head: 16 (over x, y).
Axes of the slice: x: 4, y: 4, z: 16, core: 2. Of those that a mesh axis runs over, the one named last changes fastest.
Arguments:
- queries: bfloat16 [24576, 4096], P(('dp', 'head')), may hold values from -35 to 35
- keys: bfloat16 [24576, 4096], P(('dp', 'head')), may hold values from -10 to 10
- values: bfloat16 [24576, 4096], P(('dp', 'head')), may hold values from -6 to 6
- key_tiles: int32 [64, 6], P('dp'), may hold values from 0 to 63, as said below
- key_counts: int32 [64], P('dp'), may hold values from 1 to 6, as said below
- out_weight: bfloat16 [4096, 6144], P('dp', 'head'), may hold values from -0.09375 to 0.09375
Outputs:
- projected: bfloat16 [24576, 6144], P('dp', 'head')
Inputs may be any that keep to these rules, and one draw needn't show every extreme that they name: `key_tiles`: row t lists tiles whose tile row and tile-frame each differ from those of t by at most 1; entry 0 is t itself; the first key_counts[t] entries are distinct, and the later ones repeat t. `key_counts`: at most the number of tiles whose tile row and tile-frame each differ from those of the tile by at most 1; some tile has 6 in every draw.
All inputs are finite; a program needn't handle non-finite values.
Results may differ from a plain program's by a relative error of at most 0.0056.
Values may be sent and summed in bfloat16 or wider, within the bound.
A program may use at most 64 MiB of HBM per device.

v0:
```python
import jax
import jax.numpy as jnp
from jax import lax
from jax.sharding import PartitionSpec as P

HD = 128
TILE = 384
GRID_F = 2
KMAX = 6


def with_halo(cells, sides, width):
    for axis, dim in sides:
        count = lax.axis_size(axis)
        ends = count - 1
        head = lax.slice_in_dim(cells, 0, width, axis=dim)
        tail = lax.slice_in_dim(cells, cells.shape[dim] - width, cells.shape[dim], axis=dim)
        cells = jnp.concatenate(
            [
                lax.ppermute(tail, axis, [(i, (i + 1) % count) for i in range(ends)]),
                cells,
                lax.ppermute(head, axis, [((i + 1) % count, i) for i in range(ends)]),
            ],
            axis=dim,
        )
    return cells


def local(queries, keys, values, key_tiles, key_counts, out_weight):
    query_rows, key_rows, value_rows = (
        lax.all_to_all(queries, "head", split_axis=1, concat_axis=0, tiled=True),
        lax.all_to_all(keys, "head", split_axis=1, concat_axis=0, tiled=True),
        lax.all_to_all(values, "head", split_axis=1, concat_axis=0, tiled=True),
    )
    columns_here = query_rows.shape[1]
    heads_here = columns_here // HD
    stacked = jnp.stack((key_rows, value_rows))
    extended = with_halo(stacked, (("dp", 1),), GRID_F * TILE)
    tiles_here = key_tiles.shape[0]
    first_tile = lax.axis_index("dp") * tiles_here
    score_scale = HD ** (-0.5)

    def tile_attention(inputs):
        local_tile, listed, live_count = inputs
        query_tile = lax.dynamic_slice_in_dim(query_rows, local_tile * TILE, TILE, 0).reshape(
            TILE, heads_here, HD
        )
        starts = (listed - first_tile + GRID_F) * TILE

        def key_block_at(block_index):
            sliced = lax.dynamic_slice_in_dim(extended, starts[block_index], TILE, 1)
            return (
                sliced[0].reshape(TILE, heads_here, HD),
                sliced[1].reshape(TILE, heads_here, HD),
            )

        key_block, value_block = jax.vmap(key_block_at)(jnp.arange(KMAX))
        key_all = key_block.reshape(KMAX * TILE, heads_here, HD)
        value_all = value_block.reshape(KMAX * TILE, heads_here, HD)
        scored = (
            jnp.einsum("qhd,khd->hqk", query_tile, key_all, preferred_element_type=jnp.float32)
            * score_scale
        )
        live_mask = jnp.repeat(jnp.arange(KMAX) < live_count, TILE)
        scored = jnp.where(live_mask[None, None, :], scored, -jnp.inf)
        peak_score = jnp.max(scored, axis=2, keepdims=True)
        weights = jnp.exp(scored - peak_score)
        denominator = jnp.sum(weights, axis=2)
        weighted = jnp.einsum(
            "hqk,khd->hqd",
            weights.astype(jnp.bfloat16),
            value_all,
            preferred_element_type=jnp.float32,
        )
        attended = (weighted / denominator[:, :, None]).astype(jnp.bfloat16)
        return jnp.transpose(attended, (1, 0, 2)).reshape(TILE, columns_here)

    per_tile = lax.map(
        tile_attention, (jnp.arange(tiles_here, dtype=jnp.int32), key_tiles, key_counts)
    )
    attended = per_tile.reshape(tiles_here * TILE, columns_here)
    weight_full = lax.all_gather(out_weight, "dp", axis=0, tiled=True)
    summed = jnp.dot(
        lax.all_gather(attended, "head", axis=1, tiled=True),
        weight_full,
        preferred_element_type=jnp.float32,
    )
    return summed.astype(jnp.bfloat16)


def solution(mesh):
    in_specs = (
        P(("dp", "head"), None),
        P(("dp", "head"), None),
        P(("dp", "head"), None),
        P("dp", None),
        P("dp"),
        P("dp", "head"),
    )
    out_specs = P("dp", "head")
    return jax.shard_map(local, mesh=mesh, in_specs=in_specs, out_specs=out_specs, check_vma=False)
```

profile of v0, /device:TPU:1, one launch (start us, length us, event | category | flops | bytes accessed | tf_op | source)
XLA Modules:
  0.0 255.5 jit_solution(17154061950819791135)
XLA Ops:
  6.5 1.8 copy.64
  8.4 7.6 %all-to-all-start.1 = ((bf16[48,16,256]{2,0,1:T(8,128)(2,1)}), bf16[48,16,256]{2,0,1:T(8,128)(2,1)S(1)}, u32[]{:S(2)}, u32[]{:S(2)}) async-start(bf16[48,16,256]{2,0,1:T(8,128)(2,1)} %bitcast.40), calls=%async_computation.1 | async-start | bytes 786432 | tf_op jit(solution)/shard_map/all_to_all | solution.py:32
  15.9 1.0 copy.63
  17.0 7.0 %all-to-all-done.1 = bf16[48,16,256]{2,0,1:T(8,128)(2,1)S(1)} async-done(((bf16[48,16,256]{2,0,1:T(8,128)(2,1)}), bf16[48,16,256]{2,0,1:T(8,128)(2,1)S(1)}, u32[]{:S(2)}, u32[]{:S(2)}) %all-to-all-start.1) | async-done | bytes 393248 | tf_op jit(solution)/shard_map/all_to_all | solution.py:32
  24.0 11.5 %all_to_all.51 = bf16[48,16,256]{2,0,1:T(8,128)(2,1)S(1)} all-to-all(bf16[48,16,256]{2,0,1:T(8,128)(2,1)S(1)} %bitcast.68), channel_id=1, replica_groups=mesh['dp'=32,'head'=16] {'head'}, dimensions={1} | all-to-all | bytes 786432 | tf_op jit(solution)/shard_map/all_to_all | solution.py:33
  35.5 7.4 %collective-permute-start = (bf16[2,768,256]{2,1,0:T(8,128)(2,1)S(1)}, bf16[2,768,256]{2,1,0:T(8,128)(2,1)S(1)}, u32[]{:S(2)}, u32[]{:S(2)}) collective-permute-start(bf16[2,768,256]{2,1,0:T(8,128)(2,1)S(1)} %pad_maximum_fusion.1), channel_id=1, source_target_pairs={{0,16},{16,32},{32,48},{48,64},{64,80},{80,96},{96,112},{112,128},... | collective-permute-start | bytes 2359304 | tf_op jit(solution)/shard_map/ppermute | solution.py:20
  42.9 1.9 collective-permute-start.1
  45.6 4.2 %all-to-all-start = ((bf16[48,16,256]{2,0,1:T(8,128)(2,1)}), bf16[48,16,256]{2,0,1:T(8,128)(2,1)}, u32[]{:S(2)}, u32[]{:S(2)}) async-start(bf16[48,16,256]{2,0,1:T(8,128)(2,1)} %bitcast.41), calls=%async_computation | async-start | bytes 786432 | tf_op jit(solution)/shard_map/all_to_all | solution.py:31
  50.6 1.2 collective-permute-done
  51.8 4.8 %collective-permute-done.1 = bf16[2,768,256]{2,1,0:T(8,128)(2,1)S(1)} collective-permute-done((bf16[2,768,256]{2,1,0:T(8,128)(2,1)S(1)}, bf16[2,768,256]{2,1,0:T(8,128)(2,1)S(1)}, u32[]{:S(2)}, u32[]{:S(2)}) %collective-permute-start.1) | collective-permute-done | bytes 786464 | tf_op jit(solution)/shard_map/ppermute | solution.py:22
  56.8 15.7 %copy.41 = bf16[2,2304,256]{2,0,1:T(2,128)(2,1)} copy(bf16[2,2304,256]{2,1,0:T(8,128)(2,1)S(1)} %pad_maximum_fusion) | data formatting | bytes 4718592 | tf_op jit(solution)/shard_map/while | solution.py:78
  72.5 85.4 %while.10 = (s32[]{:T(128)}, bf16[2,384,256]{2,1,0:T(8,128)(2,1)}, s32[2]{0:T(128)S(1)}, s32[2]{0:T(128)S(1)}, bf16[768,256]{1,0:T(8,128)(2,1)}, /*index=5*/s32[...) while((s32[]{:T(128)}, bf16[2,384,256]{2,1,0:T(8,128)(2,1)}, ...), condition=%wide.region_3.4_spmd, body=%wide.region_0.3_spmd.sunk | while | flops 925630016 | bytes 71205968 | solution.py:78
  73.9 1.0 constant_dynamic-slice_fusion.3
  74.9 0.8 copy.72
  76.4 9.5 %gather_fusion.1 = bf16[6,2,384,256]{3,1,2,0:T(2,128)(2,1)S(1)} fusion(bf16[2,2304,256]{2,0,1:T(2,128)(2,1)} %get-tuple-element.188, s32[6]{0:T(128)S(1)} %fusion.42), kind=kCustom, calls=%fused_computation.1.clone.1 | custom fusion | bytes 4718664 | tf_op jit(solution)/shard_map/while/body/eval_jaxpr/vmap()/gather | solution.py:51
  85.9 13.8 %slice_reduce_fusion.3 = (bf16[6,384,256]{2,1,0:T(8,128)(2,1)}, bf16[6,384,256]{2,1,0:T(8,128)(2,1)S(1)}) fusion(bf16[6,2,384,256]{3,1,2,0:T(2,128)(2,1)S(1)} %gather_fusion.1), kind=kLoop, calls=%fused_computation.10.clone.1 | loop fusion | bytes 4718592 | tf_op jit(solution)/shard_map/while/body/eval_jaxpr/vmap()/slice | solution.py:53
  99.7 2.8 %squeeze.17 = bf16[2304,2,128]{2,1,0:T(2,128)(2,1)S(1)} reshape(bf16[6,384,256]{2,1,0:T(8,128)(2,1)} %get-tuple-element.154) | data formatting | bytes 2359296 | tf_op jit(solution)/shard_map/while/body/eval_jaxpr/reshape;while/body/eval_jaxpr/vmap()/reshape;while/body/eval_jaxpr/vmap()/squeeze | solution.py:58
  103.9 2.4 fusion.43
  106.3 1.5 fusion.44
  107.8 1.4 copy-done
  109.5 4.8 %fusion.45 = bf16[384,2,128]{0,2,1:T(8,128)(2,1)S(1)} fusion(bf16[2304,2,128]{2,1,0:T(2,128)(2,1)S(1)} %squeeze.16, f32[2,384,2304]{2,1,0:T(8,128)} %copy-done, f32[2,384]{1,0:T(2,128)S(1)} %get-tuple-element.156, pred[2304]{0:T(1024)(128)(4,1)S(1)} %broadcast_in_dim.66, f32[384,2]{0,1:T(2,128)S(1)} %bitcast.73), kind=kOutput, calls=%fused_computation.16.clone.1 | convolution fusion | flops 460259328 | bytes 8462592 | tf_op jit(solution)/shard_map/while/body/eval_jaxpr/hqk,khd->hqd/dot_general | solution.py:69
  116.6 0.9 constant_dynamic-slice_fusion.3
  117.5 0.8 copy.72
  119.0 9.5 %gather_fusion.1 = bf16[6,2,384,256]{3,1,2,0:T(2,128)(2,1)S(1)} fusion(bf16[2,2304,256]{2,0,1:T(2,128)(2,1)} %get-tuple-element.188, s32[6]{0:T(128)S(1)} %fusion.42), kind=kCustom, calls=%fused_computation.1.clone.1 | custom fusion | bytes 4718664 | tf_op jit(solution)/shard_map/while/body/eval_jaxpr/vmap()/gather | solution.py:51
  128.5 13.8 %slice_reduce_fusion.3 = (bf16[6,384,256]{2,1,0:T(8,128)(2,1)}, bf16[6,384,256]{2,1,0:T(8,128)(2,1)S(1)}) fusion(bf16[6,2,384,256]{3,1,2,0:T(2,128)(2,1)S(1)} %gather_fusion.1), kind=kLoop, calls=%fused_computation.10.clone.1 | loop fusion | bytes 4718592 | tf_op jit(solution)/shard_map/while/body/eval_jaxpr/vmap()/slice | solution.py:53
  142.4 2.8 %squeeze.17 = bf16[2304,2,128]{2,1,0:T(2,128)(2,1)S(1)} reshape(bf16[6,384,256]{2,1,0:T(8,128)(2,1)} %get-tuple-element.154) | data formatting | bytes 2359296 | tf_op jit(solution)/shard_map/while/body/eval_jaxpr/reshape;while/body/eval_jaxpr/vmap()/reshape;while/body/eval_jaxpr/vmap()/squeeze | solution.py:58
  146.5 2.4 fusion.43
  148.9 1.5 fusion.44
  150.4 1.4 copy-done
  152.1 4.8 %fusion.45 = bf16[384,2,128]{0,2,1:T(8,128)(2,1)S(1)} fusion(bf16[2304,2,128]{2,1,0:T(2,128)(2,1)S(1)} %squeeze.16, f32[2,384,2304]{2,1,0:T(8,128)} %copy-done, f32[2,384]{1,0:T(2,128)S(1)} %get-tuple-element.156, pred[2304]{0:T(1024)(128)(4,1)S(1)} %broadcast_in_dim.66, f32[384,2]{0,1:T(2,128)S(1)} %bitcast.73), kind=kOutput, calls=%fused_computation.16.clone.1 | convolution fusion | flops 460259328 | bytes 8462592 | tf_op jit(solution)/shard_map/while/body/eval_jaxpr/hqk,khd->hqd/dot_general | solution.py:69
  157.9 82.9 %all-gather.3.cloned.1.call-done = bf16[768,4096]{1,0:T(8,128)(2,1)} async-done(((bf16[768,256]{1,0:T(8,128)(2,1)}), bf16[768,4096]{1,0:T(8,128)(2,1)}) %all-gather.3.cloned.1.call-update) | async-done | bytes 6291472 | tf_op jit(solution)/shard_map/all_gather | solution.py:84
  240.8 7.9 %convolution_convert_fusion = bf16[768,384]{1,0:T(8,128)(2,1)} fusion(bf16[768,4096]{1,0:T(8,128)(2,1)} %all-gather.3.cloned.1.call-done, bf16[4096,384]{1,0:T(8,128)(2,1)} %all-gather.5.cloned.1.call-done), kind=kOutput, calls=%fused_computation.32 | convolution fusion | flops 2416214016 | bytes 10027008 | tf_op jit(solution)/shard_map/dot_general | solution.py:83
  (53 shorter events, 9.6 us)
Async XLA Ops:
  6.5 38.3 %copy-start.1 = (bf16[48,4096]{1,0:T(8,128)(2,1)S(1)}, bf16[48,4096]{1,0:T(8,128)(2,1)}, u32[]{:S(2)}) copy-start(bf16[48,4096]{1,0:T(8,128)(2,1)} %param.8) | copy-start | bytes 1179652
  8.4 15.6 %all-to-all-start.1 = ((bf16[48,16,256]{2,0,1:T(8,128)(2,1)}), bf16[48,16,256]{2,0,1:T(8,128)(2,1)S(1)}, u32[]{:S(2)}, u32[]{:S(2)}) async-start(bf16[48,16,256]{2,0,1:T(8,128)(2,1)} %bitcast.40), calls=%async_computation.1 | async-start | bytes 786432 | tf_op jit(solution)/shard_map/all_to_all | solution.py:32
  35.5 16.3 %collective-permute-start = (bf16[2,768,256]{2,1,0:T(8,128)(2,1)S(1)}, bf16[2,768,256]{2,1,0:T(8,128)(2,1)S(1)}, u32[]{:S(2)}, u32[]{:S(2)}) collective-permute-start(bf16[2,768,256]{2,1,0:T(8,128)(2,1)S(1)} %pad_maximum_fusion.1), channel_id=1, source_target_pairs={{0,16},{16,32},{32,48},{48,64},{64,80},{80,96},{96,112},{112,128},... | collective-permute-start | bytes 2359304 | tf_op jit(solution)/shard_map/ppermute | solution.py:20
  42.9 13.7 %collective-permute-start.1 = (bf16[2,768,256]{2,1,0:T(8,128)(2,1)S(1)}, bf16[2,768,256]{2,1,0:T(8,128)(2,1)S(1)}, u32[]{:S(2)}, u32[]{:S(2)}) collective-permute-start(bf16[2,768,256]{2,1,0:T(8,128)(2,1)S(1)} %pad_maximum_fusion.1), channel_id=1, source_target_pairs={{16,0},{32,16},{48,32},{64,48},{80,64},{96,80},{112,96},{128,112},... | collective-permute-start | bytes 2359304 | tf_op jit(solution)/shard_map/ppermute | solution.py:22
  45.6 26.9 %all-to-all-start = ((bf16[48,16,256]{2,0,1:T(8,128)(2,1)}), bf16[48,16,256]{2,0,1:T(8,128)(2,1)}, u32[]{:S(2)}, u32[]{:S(2)}) async-start(bf16[48,16,256]{2,0,1:T(8,128)(2,1)} %bitcast.41), calls=%async_computation | async-start | bytes 786432 | tf_op jit(solution)/shard_map/all_to_all | solution.py:31
  49.8 108.1 %all-gather.5.cloned.1.call-start = ((), (), s32[]{:S(2)}) async-start(), calls=%async_computation.4 | async-start | bytes 3244032 | tf_op jit(solution)/shard_map/all_gather | solution.py:82
  50.5 190.3 %all-gather.3.cloned.1.call-start = ((), (), s32[]{:S(2)}) async-start(), calls=%async_computation.3 | async-start | bytes 6684672 | tf_op jit(solution)/shard_map/all_gather | solution.py:84
  56.7 15.7 %copy-start.4 = (s32[2,6]{1,0:T(2,128)S(1)}, s32[2,6]{1,0:T(2,128)}, u32[]{:S(2)}) copy-start(s32[2,6]{1,0:T(2,128)} %param.11) | copy-start | bytes 148
  56.7 15.7 %copy-start.5 = (s32[2]{0:T(128)S(1)}, s32[2]{0:T(128)}, u32[]{:S(2)}) copy-start(s32[2]{0:T(128)} %param.12) | copy-start | bytes 28
  106.3 2.9 %copy-start = (f32[2,384,2304]{2,1,0:T(8,128)}, f32[2,384,2304]{2,1,0:T(8,128)S(1)}, u32[]{:S(2)}) copy-start(f32[2,384,2304]{2,1,0:T(8,128)S(1)} %get-tuple-element.155) | copy-start | bytes 21233668 | tf_op jit(solution)/shard_map/while
  109.5 5.0 %copy-start.2 = (bf16[2,384,256]{2,1,0:T(8,128)(2,1)S(1)}, bf16[2,384,256]{2,1,0:T(8,128)(2,1)}, u32[]{:S(2)}) copy-start(bf16[2,384,256]{2,1,0:T(8,128)(2,1)} %get-tuple-element.170) | copy-start | bytes 1179652 | tf_op jit(solution)/shard_map/while
  114.5 0.7 copy-start.3
  148.9 2.9 %copy-start = (f32[2,384,2304]{2,1,0:T(8,128)}, f32[2,384,2304]{2,1,0:T(8,128)S(1)}, u32[]{:S(2)}) copy-start(f32[2,384,2304]{2,1,0:T(8,128)S(1)} %get-tuple-element.155) | copy-start | bytes 21233668 | tf_op jit(solution)/shard_map/while
  152.1 5.0 %copy-start.2 = (bf16[2,384,256]{2,1,0:T(8,128)(2,1)S(1)}, bf16[2,384,256]{2,1,0:T(8,128)(2,1)}, u32[]{:S(2)}) copy-start(bf16[2,384,256]{2,1,0:T(8,128)(2,1)} %get-tuple-element.170) | copy-start | bytes 1179652 | tf_op jit(solution)/shard_map/while
  157.1 0.7 copy-start.3
Sparse Core Ops, SparseCore 0:
  52.8 78.6 all-gather.4
  158.0 82.7 all-gather.2
where the time goes:
time: 256 us
  waiting for transfers between devices  96.6 us (38%)
  local copies, waits for them, and re-layouts  84.2 us (33%)
  matrix products  22.3 us (9%)
  starting transfers between devices  21.2 us (8%)
  between operations  13.5 us (5%)
  blocking collectives  11.5 us (4%)
  other arithmetic  4.6 us (2%)
    all_gather x1, waiting for transfers between devices, local(): lax.all_gather(attended, 'head', axis=1, tiled=True)  82.9 us
    slice x2, local copies, waits for them, and re-layouts, key_block_at(): sliced[0].reshape(TILE, heads_here, HD)  27.6 us
    gather x4, local copies, waits for them, and re-layouts, key_block_at(): sliced = lax.dynamic_slice_in_dim(extended, starts[block_index], TILE, 1)  20.3 us
    while x1, local copies, waits for them, and re-layouts, local(): lax.map(tile_attention, (jnp.arange(tiles_here, dtype=jnp.int32), key_til...  15.7 us
    all_to_all x1, blocking collectives, local(): lax.all_to_all(values, 'head', split_axis=1, concat_axis=0, tiled=True)  11.5 us
    dot_general x2, matrix products, tile_attention(): jnp.einsum('hqk,khd->hqd', weights.astype(jnp.bfloat16), value_all, prefe...  9.62 us
    dot_general x1, matrix products, local(): jnp.dot(lax.all_gather(attended, 'head', axis=1, tiled=True), weight_full...  7.93 us
    all_to_all x1, starting transfers between devices, local(): lax.all_to_all(keys, 'head', split_axis=1, concat_axis=0, tiled=True)  7.58 us
  transfers between devices with their start and end apart: 6, of which 4 were waited for; matrix products, arithmetic and copies ran while one was open for 38% of the time, Pallas kernels for 0%

commit v1 on v0

v1 whole, which is shorter than its diff:
```python
import math

import jax
import jax.numpy as jnp
from jax import lax
from jax.experimental import pallas as pl
from jax.experimental.pallas import tpu as pltpu
from jax.sharding import PartitionSpec as P

HD = 128
TILE = 384
KMAX = 6
GRID_F = 2
ROWS = 768
TOK = 48
PAIR = 256
COLS = 384
DEAD = 1e30
MESH = pl.DeviceIdType.MESH


def kernel(
    tiles_ref, counts_ref, q_hbm, k_hbm, v_hbm, w_hbm, out_ref,
    q_rows, k_ext, v_ext, wbuf, agat, pc, rc, acc,
    local_sem, a2a_send, a2a_recv, halo_send, halo_recv,
    xr_send, xr_recv, plus_send, plus_recv, minus_send, minus_recv, sib_send, sib_recv,
    gat_send, gat_recv, rs_send, rs_recv,
):
    dp = lax.axis_index("dp")
    h = lax.axis_index("head")
    z, c = dp // 2, dp % 2
    x, y = h // 4, h % 4
    sibling = dp + 1 - 2 * c

    def remote(src, dst, send, recv, dp_to, h_to):
        return pltpu.make_async_remote_copy(
            src_ref=src, dst_ref=dst, send_sem=send, recv_sem=recv, device_id=(dp_to, h_to), device_id_type=MESH
        )

    barrier = pltpu.get_barrier_semaphore()

    def greet(i, carry):
        pl.semaphore_signal(barrier, inc=1, device_id=(dp, (h + i) % 16), device_id_type=MESH)
        return carry

    lax.fori_loop(1, 16, greet, 0)
    for step in (1, 2, 30, 31):
        pl.semaphore_signal(barrier, inc=1, device_id=((dp + step) % 32, h), device_id_type=MESH)
    pl.semaphore_wait(barrier, 19)

    own_rows = pl.ds(pl.multiple_of(128 * (2 * (z // 4) + c), 128), 128)
    ring_x = z % 4
    is_src = ring_x == x

    def xr_copy():
        return remote(w_hbm, wbuf.at[x, own_rows], xr_send, xr_recv.at[x], dp, 4 * ring_x + y)

    w_local = pltpu.make_async_copy(w_hbm, wbuf.at[x, own_rows], local_sem.at[3])

    @pl.when(is_src)
    def _():
        w_local.start()

    @pl.when(jnp.logical_not(is_src))
    def _():
        xr_copy().start()

    sources = (k_hbm, v_hbm, q_hbm)
    targets = (k_ext, v_ext, q_rows)
    bases = (ROWS, ROWS, 0)

    def columns_of(head_to):
        return pl.ds(pl.multiple_of(PAIR * (head_to // 4 + 4 * (head_to % 4)), PAIR), PAIR)

    def land(a, head_from):
        return targets[a].at[pl.ds(pl.multiple_of(bases[a] + TOK * head_from, 16), TOK)]

    def a2a_copy(a, i):
        to = (h + i) % 16
        return remote(sources[a].at[:, columns_of(to)], land(a, h), a2a_send.at[a, i], a2a_recv.at[a, i], dp, to)

    def own_copy(a):
        return pltpu.make_async_copy(sources[a].at[:, columns_of(h)], land(a, h), local_sem.at[a])

    for a in range(3):
        own_copy(a).start()

        def start_one(i, carry, a=a):
            a2a_copy(a, i).start()
            return carry

        lax.fori_loop(1, 16, start_one, 0)

    def a2a_wait(a):
        own_copy(a).wait()

        def wait_one(i, carry):
            a2a_copy(a, i).wait_recv()
            return carry

        lax.fori_loop(1, 16, wait_one, 0)

    middle = pl.ds(ROWS, ROWS)
    sides = (pl.ds(0, ROWS), pl.ds(2 * ROWS, ROWS))

    def halo_copy(a, side):
        return remote(
            targets[a].at[middle], targets[a].at[sides[side]], halo_send.at[a, side], halo_recv.at[a, side],
            (dp + 1 + 30 * side) % 32, h,
        )

    has_next, has_prev = dp < 31, dp > 0

    def halo_start(a):
        @pl.when(has_next)
        def _():
            halo_copy(a, 0).start()

        @pl.when(has_prev)
        def _():
            halo_copy(a, 1).start()

    def halo_wait_recv(a):
        @pl.when(has_prev)
        def _():
            halo_copy(a, 0).wait_recv()

        @pl.when(has_next)
        def _():
            halo_copy(a, 1).wait_recv()

    def halo_wait_send(a):
        @pl.when(has_next)
        def _():
            halo_copy(a, 0).wait_send()

        @pl.when(has_prev)
        def _():
            halo_copy(a, 1).wait_send()

    @pl.when(jnp.logical_not(has_prev))
    def _():
        k_ext[0:ROWS, :] = jnp.zeros((ROWS, PAIR), jnp.bfloat16)
        v_ext[0:ROWS, :] = jnp.zeros((ROWS, PAIR), jnp.bfloat16)

    @pl.when(jnp.logical_not(has_next))
    def _():
        k_ext[2 * ROWS : 3 * ROWS, :] = jnp.zeros((ROWS, PAIR), jnp.bfloat16)
        v_ext[2 * ROWS : 3 * ROWS, :] = jnp.zeros((ROWS, PAIR), jnp.bfloat16)

    ahead = (z - x + 16) % 4
    behind = (x - z + 16) % 4
    ahead_from = (ahead + 3) % 4 + 1
    behind_from = (behind + 3) % 4 + 1
    dp_plus, dp_minus = (dp + 2) % 32, (dp + 30) % 32

    def block(j, zs):
        return wbuf.at[j, pl.ds(pl.multiple_of(128 * (2 * (zs // 4) + c), 128), 128)]

    def plus_copy(i):
        b = block(i % 4, (z - ahead - 4 * (i // 4) + 32) % 16)
        return remote(b, b, plus_send.at[i], plus_recv.at[i], dp_plus, h)

    def plus_arrival(i):
        b = block(i % 4, (z - ahead_from - 4 * (i // 4) + 32) % 16)
        return remote(b, b, plus_send.at[i], plus_recv.at[i], dp_plus, h)

    def minus_copy(i):
        b = block(i % 4, (z + behind + 4 * (i // 4)) % 16)
        return remote(b, b, minus_send.at[i], minus_recv.at[i], dp_minus, h)

    def minus_arrival(i):
        b = block(i % 4, (z + behind_from + 4 * (i // 4)) % 16)
        return remote(b, b, minus_send.at[i], minus_recv.at[i], dp_minus, h)

    def share(j, zs, n):
        b = block(j, zs)
        return remote(b, b, sib_send.at[n], sib_recv.at[n], sibling, h)

    def share_block(j, zs):
        return share(j, zs, 4 * (zs // 4) + j)

    def pump(i):
        @pl.when(is_src)
        def _():
            if i < 4:
                @pl.when(x == i)
                def _():
                    w_local.wait()

                @pl.when(x != i)
                def _():
                    b = block(i, z)
                    remote(b, b, xr_send, xr_recv.at[i], dp, h).wait_recv()

                share_block(i, z).start()
                plus_copy(i).start()
                minus_copy(i).start()
            else:
                plus_arrival(i - 4).wait_recv()
                plus_copy(i).start()
                share_block(i % 4, (z - 4 + 16) % 16).start()
                minus_arrival(i - 4).wait_recv()
                minus_copy(i).start()
                share_block(i % 4, (z + 4) % 16).start()

        @pl.when(jnp.logical_not(is_src))
        def _():
            plus_arrival(i).wait_recv()
            plus_copy(i).start()
            share_block(i % 4, (z - ahead_from - 4 * (i // 4) + 32) % 16).start()
            minus_arrival(i).wait_recv()
            if i < 4:
                minus_copy(i).start()
            else:
                @pl.when(behind != 3)
                def _():
                    minus_copy(i).start()

            share_block(i % 4, (z + behind_from + 4 * (i // 4)) % 16).start()

    def pump_last():
        @pl.when(is_src)
        def _():
            for i in range(4, 8):
                plus_arrival(i).wait_recv()
                share_block(i % 4, (z + 8) % 16).start()

        other = 1 - c
        for n in range(16):
            b = wbuf.at[n % 4, pl.ds(pl.multiple_of(128 * (2 * (n // 4) + other), 128), 128)]
            remote(b, b, sib_send.at[n], sib_recv.at[n], sibling, h).wait_recv()

    factor = HD ** -0.5 * math.log2(math.e)

    def bias_of(t):
        count = counts_ref[t]
        out = []
        for b in range(KMAX):
            tile = GRID_F * dp - GRID_F + b
            live = jnp.zeros((), jnp.bool_)
            for j in range(KMAX):
                live = live | ((tiles_ref[t, j] == tile) & (j < count))
            out.append(jnp.where(live, 0.0, -DEAD).astype(jnp.float32))
        return out

    def attend(t, hd, bias):
        lanes = slice(hd * HD, hd * HD + HD)
        out_lanes = pl.ds(pl.multiple_of(PAIR * y + HD * hd, HD), HD)
        for part in range(3):
            lo = t * TILE + part * 128
            q = q_rows[lo : lo + 128, lanes]
            scored = [
                lax.dot_general(
                    q, k_ext[b * TILE : (b + 1) * TILE, lanes], (((1,), (1,)), ((), ())),
                    preferred_element_type=jnp.float32,
                )
                for b in range(KMAX)
            ]
            peak = None
            for b in range(KMAX):
                here = jnp.max(scored[b], axis=1, keepdims=True) + bias[b]
                peak = here if peak is None else jnp.maximum(peak, here)
            total, weighted = None, None
            for b in range(KMAX):
                weights = jnp.exp2((scored[b] - (peak - bias[b])) * factor)
                part_sum = jnp.sum(weights, axis=1, keepdims=True)
                part_out = jnp.dot(
                    weights.astype(jnp.bfloat16), v_ext[b * TILE : (b + 1) * TILE, lanes],
                    preferred_element_type=jnp.float32,
                )
                total = part_sum if total is None else total + part_sum
                weighted = part_out if weighted is None else weighted + part_out
            agat[lo : lo + 128, out_lanes] = (weighted / total).astype(jnp.bfloat16)

    def gat_copy(t, hd, i):
        src = agat.at[pl.ds(t * TILE, TILE), pl.ds(pl.multiple_of(PAIR * y + HD * hd, HD), HD)]
        return remote(
            src, src, gat_send.at[2 * t + hd, i], gat_recv.at[2 * t + hd, i], dp, 4 * x + (y + i) % 4
        )

    def gat_arrival(t, hd, i):
        dst = agat.at[pl.ds(t * TILE, TILE), pl.ds(pl.multiple_of(PAIR * ((y + 4 - i) % 4) + HD * hd, HD), HD)]
        return remote(dst, dst, gat_send.at[2 * t + hd, i], gat_recv.at[2 * t + hd, i], dp, h)

    def rs_copy(t, i):
        return remote(
            pc.at[t, i - 1], rc.at[t, i - 1], rs_send.at[t, i - 1], rs_recv.at[t, i - 1], dp, 4 * ((x + i) % 4) + y
        )

    def project(t):
        for i in (2, 1, 3):
            for hd in range(2):
                gat_arrival(t, hd, i).wait_recv()
        rows = agat[t * TILE : (t + 1) * TILE, :]
        for i in (2, 1, 3, 0):
            part = jnp.dot(rows, wbuf[(x + i) % 4], preferred_element_type=jnp.float32)
            if i == 0:
                acc[t] = part
            else:
                pc[t, i - 1] = part.astype(jnp.bfloat16)
                rs_copy(t, i).start()

    def finish(t):
        summed = acc[t]
        for i in (1, 3, 2):
            rs_copy(t, i).wait_recv()
            summed = summed + rc[t, i - 1].astype(jnp.float32)
        out_ref[t * TILE : (t + 1) * TILE, :] = summed.astype(jnp.bfloat16)

    a2a_wait(0)
    halo_start(0)
    pump(0)
    a2a_wait(1)
    halo_start(1)
    pump(1)
    a2a_wait(2)
    pump(2)
    halo_wait_recv(0)
    halo_wait_recv(1)
    for t in range(2):
        bias = bias_of(t)
        for hd in range(2):
            attend(t, hd, bias)
            for i in (2, 1, 3):
                gat_copy(t, hd, i).start()
            pump(3 + 2 * t + hd)
    pump(7)
    pump_last()
    project(0)
    project(1)
    finish(0)
    finish(1)

    @pl.when(jnp.logical_not(is_src))
    def _():
        xr_copy().wait_send()

    for a in range(3):

        def sent_one(i, carry, a=a):
            a2a_copy(a, i).wait_send()
            return carry

        lax.fori_loop(1, 16, sent_one, 0)
    halo_wait_send(0)
    halo_wait_send(1)
    for i in range(8):
        plus_copy(i).wait_send()
        if i < 4:
            minus_copy(i).wait_send()
        else:
            @pl.when(behind != 3)
            def _():
                minus_copy(i).wait_send()
    for n in range(16):
        share(n % 4, 4 * (n // 4), n).wait_send()
    for t in range(2):
        for i in (1, 2, 3):
            for hd in range(2):
                gat_copy(t, hd, i).wait_send()
            rs_copy(t, i).wait_send()


def local(queries, keys, values, key_tiles, key_counts, out_weight):
    dma = pltpu.SemaphoreType.DMA
    vmem = pltpu.VMEM
    bf16 = jnp.bfloat16
    smem_spec = pl.BlockSpec(memory_space=pltpu.SMEM)
    any_spec = pl.BlockSpec(memory_space=pl.ANY)
    return pl.pallas_call(
        kernel,
        out_shape=jax.ShapeDtypeStruct((ROWS, COLS), bf16),
        in_specs=[smem_spec, smem_spec, any_spec, any_spec, any_spec, any_spec],
        out_specs=pl.BlockSpec(memory_space=pltpu.VMEM),
        scratch_shapes=[
            vmem((ROWS, PAIR), bf16),
            vmem((3 * ROWS, PAIR), bf16),
            vmem((3 * ROWS, PAIR), bf16),
            vmem((4, 1024, COLS), bf16),
            vmem((ROWS, 1024), bf16),
            vmem((2, 3, TILE, COLS), bf16),
            vmem((2, 3, TILE, COLS), bf16),
            vmem((2, TILE, COLS), jnp.float32),
            dma((4,)),
            dma((3, 16)), dma((3, 16)),
            dma((2, 2)), dma((2, 2)),
            dma, dma((4,)),
            dma((8,)), dma((8,)),
            dma((8,)), dma((8,)),
            dma((16,)), dma((16,)),
            dma((4, 4)), dma((4, 4)),
            dma((2, 3)), dma((2, 3)),
        ],
        compiler_params=pltpu.CompilerParams(
            collective_id=0, has_side_effects=True, vmem_limit_bytes=56 * 1024 * 1024
        ),
    )(key_tiles, key_counts, queries, keys, values, out_weight)


def solution(mesh):
    in_specs = (
        P(("dp", "head"), None),
        P(("dp", "head"), None),
        P(("dp", "head"), None),
        P("dp", None),
        P("dp"),
        P("dp", "head"),
    )
    out_specs = P("dp", "head")
    return jax.shard_map(local, mesh=mesh, in_specs=in_specs, out_specs=out_specs, check_vma=False)
```

time: 256 us -> 198 us (0.77)
  the two profiles are of different devices: /device:TPU:1 before, /device:TPU:57 now
where the time goes in v1:
time: 198 us
  Pallas kernels  196 us (99%)
    pallas_call x1, Pallas kernels, local(): pl.pallas_call(kernel, out_shape=jax.ShapeDtypeStruct((ROWS, COLS), bf16)...  196 us

profile of v1, /device:TPU:57, one launch (start us, length us, event | category | flops | bytes accessed | tf_op | source)
XLA Modules:
  0.0 197.5 jit_solution(8559872877066308319)
XLA Ops:
  0.0 195.6 %shard_map.64 = bf16[768,384]{1,0:T(8,128)(2,1)} custom-call(s32[2,6]{1,0:T(2,128)} %tiles_ref.1, s32[2]{0:T(128)} %counts_ref.1, bf16[48,4096]{1,0:T(8,128)(2,1)} %q_hbm.1, bf16[48,4096]{1,0:T(8,128)(2,1)} %k_hbm.1, bf16[48,4096]{1,0:T(8,128)(2,1)} %v_hbm.1, bf16[128,384]{1,0:T(8,128)(2,1)} %w_hbm.1), custom_call_target="tpu_custom_call" | custom-call | tf_op jit(solution)/shard_map/pallas_call | solution.py:371
  195.6 1.9 copy.8

commit v2 on v1

v2 whole, which is shorter than its diff:
```python
import math

import jax
import jax.numpy as jnp
from jax import lax
from jax.experimental import pallas as pl
from jax.experimental.pallas import tpu as pltpu
from jax.sharding import PartitionSpec as P

HD = 128
TILE = 384
KMAX = 6
GRID_F = 2
ROWS = 768
TOK = 48
PAIR = 256
COLS = 384
DEAD = 1e30
CHUNK = 192
CHUNKS = ROWS // CHUNK
SUBS = 2
SUB = 128 // SUBS
MESH = pl.DeviceIdType.MESH


def kernel(
    tiles_ref, counts_ref, q_hbm, k_hbm, v_hbm, w_hbm, out_ref,
    q_rows, k_ext, v_ext, wbuf, agat, pc, rc, acc,
    local_sem, a2a_send, a2a_recv, halo_send, halo_recv,
    scatter_send, scatter_recv, plus_send, plus_recv, minus_send, minus_recv, sib_send, sib_recv,
    gat_send, gat_recv, rs_send, rs_recv,
):
    dp = lax.axis_index("dp")
    h = lax.axis_index("head")
    z, c = dp // 2, dp % 2
    x, y = h // 4, h % 4
    sibling = dp + 1 - 2 * c

    def remote(src, dst, send, recv, dp_to, h_to):
        return pltpu.make_async_remote_copy(
            src_ref=src, dst_ref=dst, send_sem=send, recv_sem=recv, device_id=(dp_to, h_to), device_id_type=MESH
        )

    def ring_block(zn, core):
        k = (zn - x + 17) % 4
        zs = (zn - k + 17) % 16
        return k, pl.multiple_of(128 * (2 * (zs // 4) + core), 128)

    stays = (z % 4 == x) & (x == 1)
    scatter_dp = 2 * ((z + x + 15) % 16) + c
    scatter_h = 4 * (z % 4) + y
    from_k = (z - x + 17) % 4
    from_dp = 2 * ((z - from_k + 17) % 16) + c

    barrier = pltpu.get_barrier_semaphore()

    def greet(i, carry):
        pl.semaphore_signal(barrier, inc=1, device_id=(dp, (h + i) % 16), device_id_type=MESH)
        return carry

    lax.fori_loop(1, 16, greet, 0)
    for step in (1, 2, 30, 31):
        pl.semaphore_signal(barrier, inc=1, device_id=((dp + step) % 32, h), device_id_type=MESH)

    @pl.when(jnp.logical_not(stays))
    def _():
        pl.semaphore_signal(barrier, inc=1, device_id=(scatter_dp, scatter_h), device_id_type=MESH)
        pl.semaphore_signal(barrier, inc=1, device_id=(from_dp, 4 * from_k + y), device_id_type=MESH)
        pl.semaphore_wait(barrier, 21)

    @pl.when(stays)
    def _():
        pl.semaphore_wait(barrier, 19)

    def scatter_copy():
        dst = wbuf.at[x, pl.ds(pl.multiple_of(128 * (2 * (z // 4) + c), 128), 128)]
        return remote(w_hbm, dst, scatter_send, scatter_recv, scatter_dp, scatter_h)

    first_k, first_row = ring_block(z, c)
    first = wbuf.at[first_k, pl.ds(first_row, 128)]
    w_local = pltpu.make_async_copy(w_hbm, first, local_sem.at[3])

    @pl.when(stays)
    def _():
        w_local.start()

    @pl.when(jnp.logical_not(stays))
    def _():
        scatter_copy().start()

    sources = (k_hbm, v_hbm, q_hbm)
    targets = (k_ext, v_ext, q_rows)
    bases = (ROWS, ROWS, 0)

    def columns_of(head_to):
        return pl.ds(pl.multiple_of(PAIR * (head_to // 4 + 4 * (head_to % 4)), PAIR), PAIR)

    def land(a, head_from):
        return targets[a].at[pl.ds(pl.multiple_of(bases[a] + TOK * head_from, 16), TOK)]

    def a2a_copy(a, i):
        to = (h + i) % 16
        return remote(sources[a].at[:, columns_of(to)], land(a, h), a2a_send.at[a, i], a2a_recv.at[a, i], dp, to)

    def own_copy(a):
        return pltpu.make_async_copy(sources[a].at[:, columns_of(h)], land(a, h), local_sem.at[a])

    for a in range(3):
        own_copy(a).start()

        def start_one(i, carry, a=a):
            a2a_copy(a, i).start()
            return carry

        lax.fori_loop(1, 16, start_one, 0)

    def a2a_wait(a):
        own_copy(a).wait()

        def wait_one(i, carry):
            a2a_copy(a, i).wait_recv()
            return carry

        lax.fori_loop(1, 16, wait_one, 0)

    middle = pl.ds(ROWS, ROWS)
    sides = (pl.ds(0, ROWS), pl.ds(2 * ROWS, ROWS))

    def halo_copy(a, side):
        return remote(
            targets[a].at[middle], targets[a].at[sides[side]], halo_send.at[a, side], halo_recv.at[a, side],
            (dp + 1 + 30 * side) % 32, h,
        )

    has_next, has_prev = dp < 31, dp > 0

    def halo_start(a):
        @pl.when(has_next)
        def _():
            halo_copy(a, 0).start()

        @pl.when(has_prev)
        def _():
            halo_copy(a, 1).start()

    def halo_wait_recv(a):
        @pl.when(has_prev)
        def _():
            halo_copy(a, 0).wait_recv()

        @pl.when(has_next)
        def _():
            halo_copy(a, 1).wait_recv()

    def halo_wait_send(a):
        @pl.when(has_next)
        def _():
            halo_copy(a, 0).wait_send()

        @pl.when(has_prev)
        def _():
            halo_copy(a, 1).wait_send()

    @pl.when(jnp.logical_not(has_prev))
    def _():
        k_ext[0:ROWS, :] = jnp.zeros((ROWS, PAIR), jnp.bfloat16)
        v_ext[0:ROWS, :] = jnp.zeros((ROWS, PAIR), jnp.bfloat16)

    @pl.when(jnp.logical_not(has_next))
    def _():
        k_ext[2 * ROWS : 3 * ROWS, :] = jnp.zeros((ROWS, PAIR), jnp.bfloat16)
        v_ext[2 * ROWS : 3 * ROWS, :] = jnp.zeros((ROWS, PAIR), jnp.bfloat16)

    dp_plus, dp_minus = (dp + 2) % 32, (dp + 30) % 32

    def piece(zn, i, core):
        k, row = ring_block(zn, core)
        return wbuf.at[k, pl.ds(pl.multiple_of(row + SUB * (i % SUBS), SUB), SUB)]

    def plus_copy(i):
        b = piece((z - i // SUBS + 16) % 16, i, c)
        return remote(b, b, plus_send.at[i], plus_recv.at[i], dp_plus, h)

    def plus_arrival(i):
        b = piece((z - 1 - i // SUBS + 16) % 16, i, c)
        return remote(b, b, plus_send.at[i], plus_recv.at[i], dp_plus, h)

    def minus_copy(i):
        b = piece((z + i // SUBS) % 16, i, c)
        return remote(b, b, minus_send.at[i], minus_recv.at[i], dp_minus, h)

    def minus_arrival(i):
        b = piece((z + 1 + i // SUBS) % 16, i, c)
        return remote(b, b, minus_send.at[i], minus_recv.at[i], dp_minus, h)

    def share(zn, i, n):
        b = piece(zn, i, c)
        return remote(b, b, sib_send.at[n], sib_recv.at[n], sibling, h)

    def share_plus(i):
        return share((z - 1 - i // SUBS + 16) % 16, i, SUBS + i)

    def share_minus(i):
        return share((z + 1 + i // SUBS) % 16, i, 9 * SUBS + i)

    def pump(step):
        if step < SUBS:
            if step == 0:
                @pl.when(stays)
                def _():
                    w_local.wait()

                @pl.when(jnp.logical_not(stays))
                def _():
                    remote(first, first, scatter_send, scatter_recv, dp, h).wait_recv()

            plus_copy(step).start()
            minus_copy(step).start()
            share(z, step, step).start()
            return
        i = step - SUBS
        if i >= 8 * SUBS:
            return
        plus_arrival(i).wait_recv()
        if i < 7 * SUBS:
            plus_copy(i + SUBS).start()
        share_plus(i).start()
        if i < 7 * SUBS:
            minus_arrival(i).wait_recv()
            if i < 6 * SUBS:
                minus_copy(i + SUBS).start()
            share_minus(i).start()

    def sibling_wait():
        other = 1 - c
        for n in range(16 * SUBS):
            if n < SUBS:
                zn = z
            elif n < 9 * SUBS:
                zn = (z - n // SUBS + 16) % 16
            else:
                zn = (z + n // SUBS - 8) % 16
            b = piece(zn, n, other)
            remote(b, b, sib_send.at[n], sib_recv.at[n], sibling, h).wait_recv()

    factor = HD ** -0.5 * math.log2(math.e)

    def bias_of(t):
        count = counts_ref[t]
        out = []
        for b in range(KMAX):
            tile = GRID_F * dp - GRID_F + b
            live = jnp.zeros((), jnp.bool_)
            for j in range(KMAX):
                live = live | ((tiles_ref[t, j] == tile) & (j < count))
            out.append(jnp.where(live, 0.0, -DEAD).astype(jnp.float32))
        return out

    def attend(chunk, hd, bias):
        lanes = slice(hd * HD, hd * HD + HD)
        out_lanes = pl.ds(pl.multiple_of(PAIR * y + HD * hd, HD), HD)
        lo = chunk * CHUNK
        q = q_rows[lo : lo + CHUNK, lanes]
        scored = [
            lax.dot_general(
                q, k_ext[b * TILE : (b + 1) * TILE, lanes], (((1,), (1,)), ((), ())),
                preferred_element_type=jnp.float32,
            )
            for b in range(KMAX)
        ]
        peak = None
        for b in range(KMAX):
            here = jnp.max(scored[b], axis=1, keepdims=True) + bias[b]
            peak = here if peak is None else jnp.maximum(peak, here)
        total, weighted = None, None
        for b in range(KMAX):
            weights = jnp.exp2((scored[b] - (peak - bias[b])) * factor)
            part_sum = jnp.sum(weights, axis=1, keepdims=True)
            part_out = jnp.dot(
                weights.astype(jnp.bfloat16), v_ext[b * TILE : (b + 1) * TILE, lanes],
                preferred_element_type=jnp.float32,
            )
            total = part_sum if total is None else total + part_sum
            weighted = part_out if weighted is None else weighted + part_out
        agat[lo : lo + CHUNK, out_lanes] = (weighted / total).astype(jnp.bfloat16)

    def gat_block(chunk, y_of):
        return agat.at[pl.ds(chunk * CHUNK, CHUNK), pl.ds(pl.multiple_of(PAIR * y_of, PAIR), PAIR)]

    def gat_copy(chunk, i):
        b = gat_block(chunk, y)
        return remote(b, b, gat_send.at[chunk, i], gat_recv.at[chunk, i], dp, 4 * x + (y + i) % 4)

    def gat_arrival(chunk, i):
        b = gat_block(chunk, (y + 4 - i) % 4)
        return remote(b, b, gat_send.at[chunk, i], gat_recv.at[chunk, i], dp, h)

    def rs_copy(chunk, i):
        return remote(
            pc.at[chunk, i - 1], rc.at[chunk, i - 1], rs_send.at[chunk, i - 1], rs_recv.at[chunk, i - 1],
            dp, 4 * ((x + i) % 4) + y,
        )

    def project(chunk):
        for i in (1, 3, 2):
            gat_arrival(chunk, i).wait_recv()
        rows = agat[chunk * CHUNK : (chunk + 1) * CHUNK, :]
        for i in (2, 1, 3, 0):
            part = jnp.dot(rows, wbuf[(x + i) % 4], preferred_element_type=jnp.float32)
            if i == 0:
                acc[chunk] = part
            else:
                pc[chunk, i - 1] = part.astype(jnp.bfloat16)
                rs_copy(chunk, i).start()

    def finish(chunk):
        summed = acc[chunk]
        for i in (1, 3, 2):
            rs_copy(chunk, i).wait_recv()
            summed = summed + rc[chunk, i - 1].astype(jnp.float32)
        out_ref[chunk * CHUNK : (chunk + 1) * CHUNK, :] = summed.astype(jnp.bfloat16)

    biases = [bias_of(0), bias_of(1)]

    def attention(chunk, pumps):
        for hd in range(2):
            attend(chunk, hd, biases[chunk * CHUNK // TILE])
            for step in pumps[hd]:
                pump(step)
        for i in (2, 1, 3):
            gat_copy(chunk, i).start()

    pump(0)
    pump(1)
    a2a_wait(0)
    halo_start(0)
    pump(2)
    pump(3)
    a2a_wait(1)
    halo_start(1)
    for step in (4, 5, 6, 7):
        pump(step)
    a2a_wait(2)
    pump(8)
    pump(9)
    halo_wait_recv(0)
    halo_wait_recv(1)
    attention(0, ((10, 11), (12, 13)))
    attention(1, ((14, 15), (16, 17)))
    sibling_wait()
    project(0)
    attention(2, ((), ()))
    project(1)
    attention(3, ((), ()))
    project(2)
    project(3)
    for chunk in range(CHUNKS):
        finish(chunk)

    @pl.when(jnp.logical_not(stays))
    def _():
        scatter_copy().wait_send()

    for a in range(3):

        def sent_one(i, carry, a=a):
            a2a_copy(a, i).wait_send()
            return carry

        lax.fori_loop(1, 16, sent_one, 0)
    halo_wait_send(0)
    halo_wait_send(1)
    for i in range(8 * SUBS):
        plus_copy(i).wait_send()
        share_plus(i).wait_send()
        if i < 7 * SUBS:
            minus_copy(i).wait_send()
            share_minus(i).wait_send()
    for i in range(SUBS):
        share(z, i, i).wait_send()
    for chunk in range(CHUNKS):
        for i in (1, 2, 3):
            gat_copy(chunk, i).wait_send()
            rs_copy(chunk, i).wait_send()


def local(queries, keys, values, key_tiles, key_counts, out_weight):
    dma = pltpu.SemaphoreType.DMA
    vmem = pltpu.VMEM
    bf16 = jnp.bfloat16
    smem_spec = pl.BlockSpec(memory_space=pltpu.SMEM)
    any_spec = pl.BlockSpec(memory_space=pl.ANY)
    return pl.pallas_call(
        kernel,
        out_shape=jax.ShapeDtypeStruct((ROWS, COLS), bf16),
        in_specs=[smem_spec, smem_spec, any_spec, any_spec, any_spec, any_spec],
        out_specs=pl.BlockSpec(memory_space=pltpu.VMEM),
        scratch_shapes=[
            vmem((ROWS, PAIR), bf16),
            vmem((3 * ROWS, PAIR), bf16),
            vmem((3 * ROWS, PAIR), bf16),
            vmem((4, 1024, COLS), bf16),
            vmem((ROWS, 1024), bf16),
            vmem((CHUNKS, 3, CHUNK, COLS), bf16),
            vmem((CHUNKS, 3, CHUNK, COLS), bf16),
            vmem((CHUNKS, CHUNK, COLS), jnp.float32),
            dma((4,)),
            dma((3, 16)), dma((3, 16)),
            dma((2, 2)), dma((2, 2)),
            dma, dma,
            dma((8 * SUBS,)), dma((8 * SUBS,)),
            dma((7 * SUBS,)), dma((7 * SUBS,)),
            dma((16 * SUBS,)), dma((16 * SUBS,)),
            dma((CHUNKS, 4)), dma((CHUNKS, 4)),
            dma((CHUNKS, 3)), dma((CHUNKS, 3)),
        ],
        compiler_params=pltpu.CompilerParams(
            collective_id=0, has_side_effects=True, vmem_limit_bytes=56 * 1024 * 1024
        ),
    )(key_tiles, key_counts, queries, keys, values, out_weight)


def solution(mesh):
    in_specs = (
        P(("dp", "head"), None),
        P(("dp", "head"), None),
        P(("dp", "head"), None),
        P("dp", None),
        P("dp"),
        P("dp", "head"),
    )
    out_specs = P("dp", "head")
    return jax.shard_map(local, mesh=mesh, in_specs=in_specs, out_specs=out_specs, check_vma=False)
```

time: 198 us -> 92.5 us (0.47)
  the two profiles are of different devices: /device:TPU:57 before, /device:TPU:1 now
where the time goes in v2:
time: 92.5 us; the launch traced here: 92.3 us
  Pallas kernels  90.3 us (98%)
  local copies, waits for them, and re-layouts  1.94 us (2%)
    pallas_call x1, Pallas kernels, local(): pl.pallas_call(kernel, out_shape=jax.ShapeDtypeStruct((ROWS, COLS), bf16)...  90.3 us
    unnamed x1, local copies, waits for them, and re-layouts  1.94 us

profile of v2, /device:TPU:1, one launch (start us, length us, event | category | flops | bytes accessed | tf_op | source)
XLA Modules:
  0.0 92.3 jit_solution(16784563856077589152)
XLA Ops:
  0.0 90.3 %shard_map.64 = bf16[768,384]{1,0:T(8,128)(2,1)} custom-call(s32[2,6]{1,0:T(2,128)} %tiles_ref.1, s32[2]{0:T(128)} %counts_ref.1, bf16[48,4096]{1,0:T(8,128)(2,1)} %q_hbm.1, bf16[48,4096]{1,0:T(8,128)(2,1)} %k_hbm.1, bf16[48,4096]{1,0:T(8,128)(2,1)} %v_hbm.1, bf16[128,384]{1,0:T(8,128)(2,1)} %w_hbm.1), custom_call_target="tpu_custom_call" | custom-call | tf_op jit(solution)/shard_map/pallas_call | solution.py:393
  90.4 1.9 %copy.8 = bf16[768,384]{1,0:T(8,128)(2,1)} copy(bf16[768,384]{1,0:T(8,128)(2,1)} %shard_map.64) | data formatting | bytes 1179648

commit v3 on v2

--- a/solution.py
+++ b/solution.py
@@ -18,8 +18,6 @@
 DEAD = 1e30
 CHUNK = 192
 CHUNKS = ROWS // CHUNK
-SUBS = 2
-SUB = 128 // SUBS
 MESH = pl.DeviceIdType.MESH
 
 
@@ -27,7 +25,7 @@
     tiles_ref, counts_ref, q_hbm, k_hbm, v_hbm, w_hbm, out_ref,
     q_rows, k_ext, v_ext, wbuf, agat, pc, rc, acc,
     local_sem, a2a_send, a2a_recv, halo_send, halo_recv,
-    scatter_send, scatter_recv, plus_send, plus_recv, minus_send, minus_recv, sib_send, sib_recv,
+    scatter_send, scatter_recv, plus_send, plus_recv, minus_send, minus_recv, up_send, up_recv, down_send, down_recv, sib_send, sib_recv,
     gat_send, gat_recv, rs_send, rs_recv,
 ):
     dp = lax.axis_index("dp")
@@ -59,18 +57,18 @@
         return carry
 
     lax.fori_loop(1, 16, greet, 0)
-    for step in (1, 2, 30, 31):
+    for step in (1, 2, 4, 28, 30, 31):
         pl.semaphore_signal(barrier, inc=1, device_id=((dp + step) % 32, h), device_id_type=MESH)
 
     @pl.when(jnp.logical_not(stays))
     def _():
         pl.semaphore_signal(barrier, inc=1, device_id=(scatter_dp, scatter_h), device_id_type=MESH)
         pl.semaphore_signal(barrier, inc=1, device_id=(from_dp, 4 * from_k + y), device_id_type=MESH)
+        pl.semaphore_wait(barrier, 23)
+
+    @pl.when(stays)
+    def _():
         pl.semaphore_wait(barrier, 21)
-
-    @pl.when(stays)
-    def _():
-        pl.semaphore_wait(barrier, 19)
 
     def scatter_copy():
         dst = wbuf.at[x, pl.ds(pl.multiple_of(128 * (2 * (z // 4) + c), 128), 128)]
@@ -171,76 +169,68 @@
         k_ext[2 * ROWS : 3 * ROWS, :] = jnp.zeros((ROWS, PAIR), jnp.bfloat16)
         v_ext[2 * ROWS : 3 * ROWS, :] = jnp.zeros((ROWS, PAIR), jnp.bfloat16)
 
-    dp_plus, dp_minus = (dp + 2) % 32, (dp + 30) % 32
-
-    def piece(zn, i, core):
-        k, row = ring_block(zn, core)
-        return wbuf.at[k, pl.ds(pl.multiple_of(row + SUB * (i % SUBS), SUB), SUB)]
-
-    def plus_copy(i):
-        b = piece((z - i // SUBS + 16) % 16, i, c)
-        return remote(b, b, plus_send.at[i], plus_recv.at[i], dp_plus, h)
-
-    def plus_arrival(i):
-        b = piece((z - 1 - i // SUBS + 16) % 16, i, c)
-        return remote(b, b, plus_send.at[i], plus_recv.at[i], dp_plus, h)
-
-    def minus_copy(i):
-        b = piece((z + i // SUBS) % 16, i, c)
-        return remote(b, b, minus_send.at[i], minus_recv.at[i], dp_minus, h)
-
-    def minus_arrival(i):
-        b = piece((z + 1 + i // SUBS) % 16, i, c)
-        return remote(b, b, minus_send.at[i], minus_recv.at[i], dp_minus, h)
-
-    def share(zn, i, n):
-        b = piece(zn, i, c)
+    def piece(offset, core):
+        k, row = ring_block((z + offset + 16) % 16, core)
+        return wbuf.at[k, pl.ds(row, 128)]
+
+    def along(offset, sends, recvs, n, step):
+        b = piece(offset, c)
+        return remote(b, b, sends.at[n], recvs.at[n], (dp + 2 * step + 32) % 32, h)
+
+    def plus_copy(n):
+        return along(-2 * n, plus_send, plus_recv, n, 2)
+
+    def minus_copy(n):
+        return along(2 * n, minus_send, minus_recv, n, -2)
+
+    def up_copy(n):
+        return along(-2 * n, up_send, up_recv, n, 1)
+
+    def down_copy(n):
+        return along(2 * n, down_send, down_recv, n, -1)
+
+    def share(offset):
+        b = piece(offset, c)
+        n = (offset + 16) % 16
         return remote(b, b, sib_send.at[n], sib_recv.at[n], sibling, h)
 
-    def share_plus(i):
-        return share((z - 1 - i // SUBS + 16) % 16, i, SUBS + i)
-
-    def share_minus(i):
-        return share((z + 1 + i // SUBS) % 16, i, 9 * SUBS + i)
-
-    def pump(step):
-        if step < SUBS:
-            if step == 0:
-                @pl.when(stays)
-                def _():
-                    w_local.wait()
-
-                @pl.when(jnp.logical_not(stays))
-                def _():
-                    remote(first, first, scatter_send, scatter_recv, dp, h).wait_recv()
-
-            plus_copy(step).start()
-            minus_copy(step).start()
-            share(z, step, step).start()
-            return
-        i = step - SUBS
-        if i >= 8 * SUBS:
-            return
-        plus_arrival(i).wait_recv()
-        if i < 7 * SUBS:
-            plus_copy(i + SUBS).start()
-        share_plus(i).start()
-        if i < 7 * SUBS:
-            minus_arrival(i).wait_recv()
-            if i < 6 * SUBS:
-                minus_copy(i + SUBS).start()
-            share_minus(i).start()
-
-    def sibling_wait():
-        other = 1 - c
-        for n in range(16 * SUBS):
-            if n < SUBS:
-                zn = z
-            elif n < 9 * SUBS:
-                zn = (z - n // SUBS + 16) % 16
-            else:
-                zn = (z + n // SUBS - 8) % 16
-            b = piece(zn, n, other)
+    def ring_start():
+        @pl.when(stays)
+        def _():
+            w_local.wait()
+
+        @pl.when(jnp.logical_not(stays))
+        def _():
+            remote(first, first, scatter_send, scatter_recv, dp, h).wait_recv()
+
+        plus_copy(0).start()
+        minus_copy(0).start()
+        share(0).start()
+
+    def ring_step(n):
+        along(-2 * (n + 1), plus_send, plus_recv, n, 2).wait_recv()
+        if n < 3:
+            plus_copy(n + 1).start()
+        share(-2 * (n + 1)).start()
+        if n < 3:
+            along(2 * (n + 1), minus_send, minus_recv, n, -2).wait_recv()
+            if n < 2:
+                minus_copy(n + 1).start()
+            share(2 * (n + 1)).start()
+
+    def hand_on(n):
+        up_copy(n).start()
+        down_copy(n).start()
+
+    def handed(n):
+        along(-1 - 2 * n, up_send, up_recv, n, 1).wait_recv()
+        share(-1 - 2 * n).start()
+        along(1 + 2 * n, down_send, down_recv, n, -1).wait_recv()
+        share(1 + 2 * n).start()
+
+    def sibling_wait(odd):
+        for n in range(odd, 16, 2):
+            b = piece(n, 1 - c)
             remote(b, b, sib_send.at[n], sib_recv.at[n], sibling, h).wait_recv()
 
     factor = HD ** -0.5 * math.log2(math.e)
@@ -295,21 +285,30 @@
         b = gat_block(chunk, (y + 4 - i) % 4)
         return remote(b, b, gat_send.at[chunk, i], gat_recv.at[chunk, i], dp, h)
 
+    first_way = (z + 1) % 2
+
     def rs_copy(chunk, i):
         return remote(
             pc.at[chunk, i - 1], rc.at[chunk, i - 1], rs_send.at[chunk, i - 1], rs_recv.at[chunk, i - 1],
             dp, 4 * ((x + i) % 4) + y,
         )
 
-    def project(chunk):
+    def gathered(chunk):
         for i in (1, 3, 2):
             gat_arrival(chunk, i).wait_recv()
+
+    def project(chunk, late):
         rows = agat[chunk * CHUNK : (chunk + 1) * CHUNK, :]
-        for i in (2, 1, 3, 0):
+        way = first_way + late * (1 - 2 * first_way)
+        for i in (way + 2, way):
             part = jnp.dot(rows, wbuf[(x + i) % 4], preferred_element_type=jnp.float32)
-            if i == 0:
+
+            @pl.when(i == 0)
+            def _():
                 acc[chunk] = part
-            else:
+
+            @pl.when(i > 0)
+            def _():
                 pc[chunk, i - 1] = part.astype(jnp.bfloat16)
                 rs_copy(chunk, i).start()
 
@@ -322,40 +321,50 @@
 
     biases = [bias_of(0), bias_of(1)]
 
-    def attention(chunk, pumps):
+    def attention(chunk):
         for hd in range(2):
             attend(chunk, hd, biases[chunk * CHUNK // TILE])
-            for step in pumps[hd]:
-                pump(step)
         for i in (2, 1, 3):
             gat_copy(chunk, i).start()
 
-    pump(0)
-    pump(1)
+    ring_start()
     a2a_wait(0)
     halo_start(0)
-    pump(2)
-    pump(3)
+    ring_step(0)
     a2a_wait(1)
     halo_start(1)
-    for step in (4, 5, 6, 7):
-        pump(step)
+    ring_step(1)
     a2a_wait(2)
-    pump(8)
-    pump(9)
     halo_wait_recv(0)
     halo_wait_recv(1)
-    attention(0, ((10, 11), (12, 13)))
-    attention(1, ((14, 15), (16, 17)))
-    sibling_wait()
-    project(0)
-    attention(2, ((), ()))
-    project(1)
-    attention(3, ((), ()))
-    project(2)
-    project(3)
-    for chunk in range(CHUNKS):
-        finish(chunk)
+    attention(0)
+    attention(1)
+    ring_step(2)
+    attention(2)
+    attention(3)
+    hand_on(0)
+    hand_on(1)
+    hand_on(2)
+    ring_step(3)
+    hand_on(3)
+    sibling_wait(0)
+    gathered(0)
+    project(0, 0)
+    gathered(1)
+    project(1, 0)
+    gathered(2)
+    project(2, 0)
+    gathered(3)
+    project(3, 0)
+    handed(0)
+    handed(1)
+    handed(2)
+    handed(3)
+    sibling_wait(1)
+    project(0, 1)
+    project(1, 1)
+    project(2, 1)
+    project(3, 1)
 
     @pl.when(jnp.logical_not(stays))
     def _():
@@ -370,17 +379,23 @@
         lax.fori_loop(1, 16, sent_one, 0)
     halo_wait_send(0)
     halo_wait_send(1)
-    for i in range(8 * SUBS):
-        plus_copy(i).wait_send()
-        share_plus(i).wait_send()
-        if i < 7 * SUBS:
-            minus_copy(i).wait_send()
-            share_minus(i).wait_send()
-    for i in range(SUBS):
-        share(z, i, i).wait_send()
+    for n in range(4):
+        plus_copy(n).wait_send()
+        if n < 3:
+            minus_copy(n).wait_send()
+        up_copy(n).wait_send()
+        down_copy(n).wait_send()
+    for n in range(16):
+        share(n).wait_send()
     for chunk in range(CHUNKS):
         for i in (1, 2, 3):
             gat_copy(chunk, i).wait_send()
+
+    for chunk in range(CHUNKS):
+        finish(chunk)
+
+    for chunk in range(CHUNKS):
+        for i in (1, 2, 3):
             rs_copy(chunk, i).wait_send()
 
 
@@ -408,9 +423,11 @@
             dma((3, 16)), dma((3, 16)),
             dma((2, 2)), dma((2, 2)),
             dma, dma,
-            dma((8 * SUBS,)), dma((8 * SUBS,)),
-            dma((7 * SUBS,)), dma((7 * SUBS,)),
-            dma((16 * SUBS,)), dma((16 * SUBS,)),
+            dma((4,)), dma((4,)),
+            dma((3,)), dma((3,)),
+            dma((4,)), dma((4,)),
+            dma((4,)), dma((4,)),
+            dma((16,)), dma((16,)),
             dma((CHUNKS, 4)), dma((CHUNKS, 4)),
             dma((CHUNKS, 3)), dma((CHUNKS, 3)),
         ],

time: 92.5 us -> 87.1 us (0.942)
  Pallas kernels: 90.3 us -> 85 us
    pallas_call x1, Pallas kernels: 90.3 us -> 85 us  [local(): pl.pallas_call(kernel, out_shape=jax.ShapeDtypeStruct((ROWS, COLS), bf16)...]
where the time goes in v3:
time: 87.1 us; the launch traced here: 86.9 us
  Pallas kernels  85 us (98%)
  local copies, waits for them, and re-layouts  1.94 us (2%)
    pallas_call x1, Pallas kernels, local(): pl.pallas_call(kernel, out_shape=jax.ShapeDtypeStruct((ROWS, COLS), bf16)...  85 us
    unnamed x1, local copies, waits for them, and re-layouts  1.94 us

profile of v3, /device:TPU:1, one launch (start us, length us, event | category | flops | bytes accessed | tf_op | source)
XLA Modules:
  0.0 86.9 jit_solution(15900631708630104893)
XLA Ops:
  0.0 85.0 %shard_map.64 = bf16[768,384]{1,0:T(8,128)(2,1)} custom-call(s32[2,6]{1,0:T(2,128)} %tiles_ref.1, s32[2]{0:T(128)} %counts_ref.1, bf16[48,4096]{1,0:T(8,128)(2,1)} %q_hbm.1, bf16[48,4096]{1,0:T(8,128)(2,1)} %k_hbm.1, bf16[48,4096]{1,0:T(8,128)(2,1)} %v_hbm.1, bf16[128,384]{1,0:T(8,128)(2,1)} %w_hbm.1), custom_call_target="tpu_custom_call" | custom-call | tf_op jit(solution)/shard_map/pallas_call | solution.py:408
  85.0 1.9 %copy.8 = bf16[768,384]{1,0:T(8,128)(2,1)} copy(bf16[768,384]{1,0:T(8,128)(2,1)} %shard_map.64) | data formatting | bytes 1179648

commit v4 on v2

v4 whole, which is shorter than its diff:
```python
import math

import jax
import jax.numpy as jnp
from jax import lax
from jax.experimental import pallas as pl
from jax.experimental.pallas import tpu as pltpu
from jax.sharding import PartitionSpec as P

HD = 128
TILE = 384
KMAX = 6
GRID_F = 2
ROWS = 768
TOK = 48
PAIR = 256
COLS = 384
DEAD = 1e30
CHUNK = 192
CHUNKS = ROWS // CHUNK
MESH = pl.DeviceIdType.MESH


def kernel(
    tiles_ref, counts_ref, q_hbm, k_hbm, v_hbm, w_hbm, out_ref,
    q_rows, k_ext, v_ext, weight, agat,
    local_sem, a2a_send, a2a_recv, halo_send, halo_recv, known,
    far_send, far_recv, half_send, half_recv, near_send, near_recv, next_send, next_recv, sib_send, sib_recv,
    s1_send, s1_recv, s2_send, s2_recv, s3_send, s3_recv,
):
    dp = lax.axis_index("dp")
    h = lax.axis_index("head")
    z, c = dp // 2, dp % 2
    x, y = h // 4, h % 4
    sibling = dp + 1 - 2 * c

    def remote(src, dst, send, recv, dp_to, h_to):
        return pltpu.make_async_remote_copy(
            src_ref=src, dst_ref=dst, send_sem=send, recv_sem=recv, device_id=(dp_to, h_to), device_id_type=MESH
        )

    has_next, has_prev = dp < 31, dp > 0
    has_up, has_down = z < 15, z > 0
    barrier = pltpu.get_barrier_semaphore()

    def signal(sem, dp_to, h_to):
        pl.semaphore_signal(sem, inc=1, device_id=(dp_to, h_to), device_id_type=MESH)

    def greet(i, carry):
        signal(barrier, dp, (h + i) % 16)
        return carry

    lax.fori_loop(1, 16, greet, 0)
    for there, step in ((has_next, 1), (has_prev, -1), (has_up, 2), (has_down, -2)):
        @pl.when(there)
        def _():
            signal(barrier, (dp + step + 32) % 32, h)

    @pl.when(has_up & has_down)
    def _():
        pl.semaphore_wait(barrier, 19)

    @pl.when(jnp.logical_not(has_up) | jnp.logical_not(has_down))
    def _():
        @pl.when(has_next & has_prev)
        def _():
            pl.semaphore_wait(barrier, 18)

        @pl.when(jnp.logical_not(has_next) | jnp.logical_not(has_prev))
        def _():
            pl.semaphore_wait(barrier, 17)

    def meet_signal(r):
        @pl.when(z + 2**r < 16)
        def _():
            signal(known.at[r, 0], (dp + 2 ** (r + 1)) % 32, h)

        @pl.when(z >= 2**r)
        def _():
            signal(known.at[r, 1], (dp - 2 ** (r + 1) + 32) % 32, h)

    def meet_wait(r):
        @pl.when(z >= 2**r)
        def _():
            pl.semaphore_wait(known.at[r, 0], 1)

        @pl.when(z + 2**r < 16)
        def _():
            pl.semaphore_wait(known.at[r, 1], 1)

    meet_signal(0)

    sources = (k_hbm, v_hbm, q_hbm)
    targets = (k_ext, v_ext, q_rows)
    bases = (ROWS, ROWS, 0)

    def columns_of(head_to):
        return pl.ds(pl.multiple_of(PAIR * head_to, PAIR), PAIR)

    def land(a, head_from):
        return targets[a].at[pl.ds(pl.multiple_of(bases[a] + TOK * head_from, 16), TOK)]

    def a2a_copy(a, i):
        to = (h + i) % 16
        return remote(sources[a].at[:, columns_of(to)], land(a, h), a2a_send.at[a, i], a2a_recv.at[a, i], dp, to)

    def own_copy(a):
        return pltpu.make_async_copy(sources[a].at[:, columns_of(h)], land(a, h), local_sem.at[a])

    for a in range(3):
        own_copy(a).start()

        def start_one(i, carry, a=a):
            a2a_copy(a, i).start()
            return carry

        lax.fori_loop(1, 16, start_one, 0)

    def a2a_wait(a):
        own_copy(a).wait()

        def wait_one(i, carry):
            a2a_copy(a, i).wait_recv()
            return carry

        lax.fori_loop(1, 16, wait_one, 0)

    middle = pl.ds(ROWS, ROWS)
    sides = (pl.ds(0, ROWS), pl.ds(2 * ROWS, ROWS))

    def halo_copy(a, side):
        return remote(
            targets[a].at[middle], targets[a].at[sides[side]], halo_send.at[a, side], halo_recv.at[a, side],
            (dp + 1 + 30 * side) % 32, h,
        )

    def halo_start(a):
        @pl.when(has_next)
        def _():
            halo_copy(a, 0).start()

        @pl.when(has_prev)
        def _():
            halo_copy(a, 1).start()

    def halo_wait_recv(a):
        @pl.when(has_prev)
        def _():
            halo_copy(a, 0).wait_recv()

        @pl.when(has_next)
        def _():
            halo_copy(a, 1).wait_recv()

    def halo_wait_send(a):
        @pl.when(has_next)
        def _():
            halo_copy(a, 0).wait_send()

        @pl.when(has_prev)
        def _():
            halo_copy(a, 1).wait_send()

    @pl.when(jnp.logical_not(has_prev))
    def _():
        k_ext[0:ROWS, :] = jnp.zeros((ROWS, PAIR), jnp.bfloat16)
        v_ext[0:ROWS, :] = jnp.zeros((ROWS, PAIR), jnp.bfloat16)

    @pl.when(jnp.logical_not(has_next))
    def _():
        k_ext[2 * ROWS : 3 * ROWS, :] = jnp.zeros((ROWS, PAIR), jnp.bfloat16)
        v_ext[2 * ROWS : 3 * ROWS, :] = jnp.zeros((ROWS, PAIR), jnp.bfloat16)

    def weight_block(offset, core, first=0, count=128):
        return weight.at[core, pl.ds(pl.multiple_of(128 * ((z + offset + 16) % 16) + first, 64), count)]

    def along(offset, step, sends, recvs, first=0, count=128):
        b = weight_block(offset, c, first, count)
        return remote(b, b, sends, recvs, (dp + 2 * step + 32) % 32, h)

    w_local = pltpu.make_async_copy(w_hbm, weight_block(0, c), local_sem.at[3])
    w_local.start()

    def far_copy(side):
        return along(0, 4 - 8 * side, far_send.at[side], far_recv.at[side])

    def far_arrival(side):
        return along(8 * side - 4, 4 - 8 * side, far_send.at[side], far_recv.at[side])

    def far_start(wraps):
        for side, inside in ((0, z < 12), (1, z >= 4)):
            @pl.when(jnp.logical_not(inside) if wraps else inside)
            def _():
                far_copy(side).start()

    def half_copy(side):
        return along(8 * side - 4, 4 - 8 * side, half_send.at[side], half_recv.at[side], 64 * side, 64)

    def half_arrival(side):
        return along(8, 4 - 8 * side, half_send.at[side], half_recv.at[side], 64 * side, 64)

    def near_copy(m, side):
        return along(4 * m, 1 - 2 * side, near_send.at[side, m], near_recv.at[side, m])

    def near_arrival(m, side):
        return along((4 * m + 15 + 2 * side) % 16, 1 - 2 * side, near_send.at[side, m], near_recv.at[side, m])

    def next_copy(m, side):
        return along((4 * m + 15 + 2 * side) % 16, 1 - 2 * side, next_send.at[side, m], next_recv.at[side, m])

    def next_arrival(m, side):
        return along((4 * m + 14 + 4 * side) % 16, 1 - 2 * side, next_send.at[side, m], next_recv.at[side, m])

    PASSED = ((0, 3), (0, 1))

    def share(offset):
        b = weight_block(offset, c)
        return remote(b, b, sib_send.at[offset], sib_recv.at[offset], sibling, h)

    def far_pass():
        for side in range(2):
            far_arrival(side).wait_recv()
            half_copy(side).start()
        for m in (0, 3, 1):
            for side in range(2):
                near_copy(m, side).start()
        share(12).start()
        share(4).start()

    def half_pass():
        for side in range(2):
            half_arrival(side).wait_recv()
        for side in range(2):
            near_copy(2, side).start()
        share(8).start()

    def near_pass():
        for m in (0, 3, 1, 2):
            for side in range(2):
                near_arrival(m, side).wait_recv()
                if m in PASSED[side]:
                    next_copy(m, side).start()
                share((4 * m + 15 + 2 * side) % 16).start()

    def next_done():
        for side in range(2):
            for m in PASSED[side]:
                next_arrival(m, side).wait_recv()
                share((4 * m + 14 + 4 * side) % 16).start()

    def sibling_done():
        for offset in range(16):
            b = weight_block(offset, 1 - c)
            remote(b, b, sib_send.at[offset], sib_recv.at[offset], sibling, h).wait_recv()

    factor = HD ** -0.5 * math.log2(math.e)

    def bias_of(t):
        count = counts_ref[t]
        out = []
        for b in range(KMAX):
            tile = GRID_F * dp - GRID_F + b
            live = jnp.zeros((), jnp.bool_)
            for j in range(KMAX):
                live = live | ((tiles_ref[t, j] == tile) & (j < count))
            out.append(jnp.where(live, 0.0, -DEAD).astype(jnp.float32))
        return out

    def attend(chunk, hd, bias):
        lanes = slice(hd * HD, hd * HD + HD)
        out_lanes = pl.ds(pl.multiple_of(HD * h, HD), HD)
        lo = chunk * CHUNK
        q = q_rows[lo : lo + CHUNK, lanes]
        scored = [
            lax.dot_general(
                q, k_ext[b * TILE : (b + 1) * TILE, lanes], (((1,), (1,)), ((), ())),
                preferred_element_type=jnp.float32,
            )
            for b in range(KMAX)
        ]
        peak = None
        for b in range(KMAX):
            here = jnp.max(scored[b], axis=1, keepdims=True) + bias[b]
            peak = here if peak is None else jnp.maximum(peak, here)
        total, weighted = None, None
        for b in range(KMAX):
            weights = jnp.exp2((scored[b] - (peak - bias[b])) * factor)
            part_sum = jnp.sum(weights, axis=1, keepdims=True)
            part_out = jnp.dot(
                weights.astype(jnp.bfloat16), v_ext[b * TILE : (b + 1) * TILE, lanes],
                preferred_element_type=jnp.float32,
            )
            total = part_sum if total is None else total + part_sum
            weighted = part_out if weighted is None else weighted + part_out
        agat[hd, lo : lo + CHUNK, out_lanes] = (weighted / total).astype(jnp.bfloat16)

    def place(chunk, i, steps):
        if chunk % 2 == 0:
            return 4 * ((x + steps + 4) % 4) + (y - i + 4) % 4
        return 4 * ((x - i + 4) % 4) + (y + steps + 4) % 4

    def gathered_block(chunk, u):
        return agat.at[:, pl.ds(chunk * CHUNK, CHUNK), pl.ds(pl.multiple_of(HD * u, HD), HD)]

    def hop(chunk, u, to, sends, recvs):
        b = gathered_block(chunk, u)
        return remote(b, b, sends, recvs, dp, to)

    def first_copy(chunk, i):
        return hop(chunk, h, place(chunk, -i, 0), s1_send.at[chunk, i], s1_recv.at[chunk, i])

    def first_arrival(chunk, i):
        return hop(chunk, place(chunk, i, 0), h, s1_send.at[chunk, i], s1_recv.at[chunk, i])

    def second_copy(chunk, i, side):
        return hop(
            chunk, place(chunk, i, 0), place(chunk, 0, 1 - 2 * side),
            s2_send.at[chunk, side, i], s2_recv.at[chunk, side, i],
        )

    def second_arrival(chunk, i, side):
        return hop(
            chunk, place(chunk, i, 2 * side - 1), h, s2_send.at[chunk, side, i], s2_recv.at[chunk, side, i]
        )

    def third_copy(chunk, n, side):
        return hop(
            chunk, place(chunk, n + 2 * side, 2 * side - 1), place(chunk, 0, 1 - 2 * side),
            s3_send.at[chunk, side, n], s3_recv.at[chunk, side, n],
        )

    def third_arrival(chunk, n, side):
        return hop(
            chunk, place(chunk, n + 2 * side, 2), h, s3_send.at[chunk, side, n], s3_recv.at[chunk, side, n]
        )

    def send_first(chunk):
        for i in (2, 1, 3):
            first_copy(chunk, i).start()
        for side in range(2):
            second_copy(chunk, 0, side).start()

    def send_second(chunk):
        for i in (1, 3, 2):
            first_arrival(chunk, i).wait_recv()
            for side in range(2):
                second_copy(chunk, i, side).start()

    def send_third(chunk):
        for i in (0, 1, 3, 2):
            for side in range(2):
                second_arrival(chunk, i, side).wait_recv()
                if i // 2 == side:
                    third_copy(chunk, i % 2, side).start()

    def last_arrivals(chunk):
        for n in range(2):
            for side in range(2):
                third_arrival(chunk, n, side).wait_recv()

    def project(chunk):
        rows = slice(chunk * CHUNK, (chunk + 1) * CHUNK)
        out = None
        for part in range(2):
            term = jnp.dot(agat[part, rows, :], weight[part], preferred_element_type=jnp.float32)
            out = term if out is None else out + term
        out_ref[rows, :] = out.astype(jnp.bfloat16)

    biases = [bias_of(0), bias_of(1)]

    def attention(chunk):
        for hd in range(2):
            attend(chunk, hd, biases[chunk * CHUNK // TILE])
        send_first(chunk)

    meet_wait(0)
    meet_signal(1)
    a2a_wait(0)
    halo_start(0)
    meet_wait(1)
    meet_signal(2)
    a2a_wait(1)
    halo_start(1)
    w_local.wait()
    share(0).start()
    far_start(False)
    meet_wait(2)
    meet_signal(3)
    a2a_wait(2)
    meet_wait(3)
    far_start(True)
    halo_wait_recv(0)
    halo_wait_recv(1)
    attention(0)
    attention(1)
    send_second(0)
    attention(2)
    far_pass()
    attention(3)
    send_second(1)
    half_pass()
    send_third(0)
    send_second(2)
    send_third(1)
    send_second(3)
    near_pass()
    send_third(2)
    last_arrivals(0)
    send_third(3)
    last_arrivals(1)
    next_done()
    sibling_done()
    project(0)
    project(1)
    last_arrivals(2)
    project(2)
    last_arrivals(3)
    project(3)

    for a in range(3):

        def sent_one(i, carry, a=a):
            a2a_copy(a, i).wait_send()
            return carry

        lax.fori_loop(1, 16, sent_one, 0)
    halo_wait_send(0)
    halo_wait_send(1)
    for side in range(2):
        far_copy(side).wait_send()
        half_copy(side).wait_send()
        for m in range(4):
            near_copy(m, side).wait_send()
        for m in PASSED[side]:
            next_copy(m, side).wait_send()
    for offset in range(16):
        share(offset).wait_send()
    for chunk in range(CHUNKS):
        for i in range(4):
            if i > 0:
                first_copy(chunk, i).wait_send()
            for side in range(2):
                second_copy(chunk, i, side).wait_send()
                if i < 2:
                    third_copy(chunk, i, side).wait_send()


def local(queries, keys, values, key_tiles, key_counts, out_weight):
    dma = pltpu.SemaphoreType.DMA
    vmem = pltpu.VMEM
    bf16 = jnp.bfloat16
    smem_spec = pl.BlockSpec(memory_space=pltpu.SMEM)
    any_spec = pl.BlockSpec(memory_space=pl.ANY)
    return pl.pallas_call(
        kernel,
        out_shape=jax.ShapeDtypeStruct((ROWS, COLS), bf16),
        in_specs=[smem_spec, smem_spec, any_spec, any_spec, any_spec, any_spec],
        out_specs=pl.BlockSpec(memory_space=pltpu.VMEM),
        scratch_shapes=[
            vmem((ROWS, PAIR), bf16),
            vmem((3 * ROWS, PAIR), bf16),
            vmem((3 * ROWS, PAIR), bf16),
            vmem((2, 2048, COLS), bf16),
            vmem((2, ROWS, 2048), bf16),
            dma((4,)),
            dma((3, 16)), dma((3, 16)),
            dma((2, 2)), dma((2, 2)),
            pltpu.SemaphoreType.REGULAR((4, 2)),
            dma((2,)), dma((2,)),
            dma((2,)), dma((2,)),
            dma((2, 4)), dma((2, 4)),
            dma((2, 4)), dma((2, 4)),
            dma((16,)), dma((16,)),
            dma((CHUNKS, 4)), dma((CHUNKS, 4)),
            dma((CHUNKS, 2, 4)), dma((CHUNKS, 2, 4)),
            dma((CHUNKS, 2, 2)), dma((CHUNKS, 2, 2)),
        ],
        compiler_params=pltpu.CompilerParams(
            collective_id=0, has_side_effects=True, vmem_limit_bytes=56 * 1024 * 1024
        ),
    )(key_tiles, key_counts, queries, keys, values, out_weight)


def solution(mesh):
    in_specs = (
        P(("dp", "head"), None),
        P(("dp", "head"), None),
        P(("dp", "head"), None),
        P("dp", None),
        P("dp"),
        P("dp", "head"),
    )
    out_specs = P("dp", "head")
    return jax.shard_map(local, mesh=mesh, in_specs=in_specs, out_specs=out_specs, check_vma=False)
```

time: 92.5 us -> 81.1 us (0.88)
  Pallas kernels: 90.3 us -> 78.9 us
    pallas_call x1, Pallas kernels: 90.3 us -> 78.9 us  [local(): pl.pallas_call(kernel, out_shape=jax.ShapeDtypeStruct((ROWS, COLS), bf16)...]
where the time goes in v4:
time: 81.1 us; the launch traced here: 80.8 us
  Pallas kernels  78.9 us (97%)
  local copies, waits for them, and re-layouts  1.94 us (2%)
    pallas_call x1, Pallas kernels, local(): pl.pallas_call(kernel, out_shape=jax.ShapeDtypeStruct((ROWS, COLS), bf16)...  78.9 us
    unnamed x1, local copies, waits for them, and re-layouts  1.94 us

profile of v4, /device:TPU:1, one launch (start us, length us, event | category | flops | bytes accessed | tf_op | source)
XLA Modules:
  0.0 80.8 jit_solution(5801509031187362964)
XLA Ops:
  0.0 78.9 %shard_map.64 = bf16[768,384]{1,0:T(8,128)(2,1)} custom-call(s32[2,6]{1,0:T(2,128)} %tiles_ref.1, s32[2]{0:T(128)} %counts_ref.1, bf16[48,4096]{1,0:T(8,128)(2,1)} %q_hbm.1, bf16[48,4096]{1,0:T(8,128)(2,1)} %k_hbm.1, bf16[48,4096]{1,0:T(8,128)(2,1)} %v_hbm.1, bf16[128,384]{1,0:T(8,128)(2,1)} %w_hbm.1), custom_call_target="tpu_custom_call" | custom-call | tf_op jit(solution)/shard_map/pallas_call | solution.py:454
  78.9 1.9 %copy.8 = bf16[768,384]{1,0:T(8,128)(2,1)} copy(bf16[768,384]{1,0:T(8,128)(2,1)} %shard_map.64) | data formatting | bytes 1179648

commit v5 on v4

--- a/solution.py
+++ b/solution.py
@@ -107,14 +107,17 @@
     def own_copy(a):
         return pltpu.make_async_copy(sources[a].at[:, columns_of(h)], land(a, h), local_sem.at[a])
 
-    for a in range(3):
+    def a2a_start(a):
         own_copy(a).start()
 
-        def start_one(i, carry, a=a):
+        def start_one(i, carry):
             a2a_copy(a, i).start()
             return carry
 
         lax.fori_loop(1, 16, start_one, 0)
+
+    a2a_start(0)
+    a2a_start(1)
 
     def a2a_wait(a):
         own_copy(a).wait()
@@ -366,6 +369,40 @@
             out = term if out is None else out + term
         out_ref[rows, :] = out.astype(jnp.bfloat16)
 
+    def regrouped_sent():
+        for a in range(3):
+
+            def sent_one(i, carry, a=a):
+                a2a_copy(a, i).wait_send()
+                return carry
+
+            lax.fori_loop(1, 16, sent_one, 0)
+        halo_wait_send(0)
+        halo_wait_send(1)
+
+    def weight_sent():
+        for side in range(2):
+            far_copy(side).wait_send()
+            half_copy(side).wait_send()
+            for m in range(4):
+                near_copy(m, side).wait_send()
+            for m in PASSED[side]:
+                next_copy(m, side).wait_send()
+        for offset in range(16):
+            share(offset).wait_send()
+
+    def blocks_sent(chunk):
+        for i in range(4):
+            if i > 0:
+                first_copy(chunk, i).wait_send()
+            for side in range(2):
+                second_copy(chunk, i, side).wait_send()
+
+    def third_sent(chunk):
+        for n in range(2):
+            for side in range(2):
+                third_copy(chunk, n, side).wait_send()
+
     biases = [bias_of(0), bias_of(1)]
 
     def attention(chunk):
@@ -377,20 +414,21 @@
     meet_signal(1)
     a2a_wait(0)
     halo_start(0)
+    a2a_start(2)
     meet_wait(1)
     meet_signal(2)
     a2a_wait(1)
     halo_start(1)
+    meet_wait(2)
+    meet_signal(3)
     w_local.wait()
     share(0).start()
-    far_start(False)
-    meet_wait(2)
-    meet_signal(3)
     a2a_wait(2)
     meet_wait(3)
-    far_start(True)
     halo_wait_recv(0)
     halo_wait_recv(1)
+    far_start(False)
+    far_start(True)
     attention(0)
     attention(1)
     send_second(0)
@@ -407,42 +445,26 @@
     send_third(2)
     last_arrivals(0)
     send_third(3)
+    regrouped_sent()
     last_arrivals(1)
     next_done()
     sibling_done()
+    weight_sent()
     project(0)
     project(1)
+    for chunk in range(2):
+        blocks_sent(chunk)
     last_arrivals(2)
     project(2)
+    for chunk in range(2, CHUNKS):
+        blocks_sent(chunk)
+    for chunk in range(2):
+        third_sent(chunk)
     last_arrivals(3)
     project(3)
 
-    for a in range(3):
-
-        def sent_one(i, carry, a=a):
-            a2a_copy(a, i).wait_send()
-            return carry
-
-        lax.fori_loop(1, 16, sent_one, 0)
-    halo_wait_send(0)
-    halo_wait_send(1)
-    for side in range(2):
-        far_copy(side).wait_send()
-        half_copy(side).wait_send()
-        for m in range(4):
-            near_copy(m, side).wait_send()
-        for m in PASSED[side]:
-            next_copy(m, side).wait_send()
-    for offset in range(16):
-        share(offset).wait_send()
-    for chunk in range(CHUNKS):
-        for i in range(4):
-            if i > 0:
-                first_copy(chunk, i).wait_send()
-            for side in range(2):
-                second_copy(chunk, i, side).wait_send()
-                if i < 2:
-                    third_copy(chunk, i, side).wait_send()
+    for chunk in range(2, CHUNKS):
+        third_sent(chunk)
 
 
 def local(queries, keys, values, key_tiles, key_counts, out_weight):

time: 81.1 us -> 81.2 us (level)
  no operation moved by 1% of the time
where the time goes in v5:
time: 81.2 us; the launch traced here: 80.4 us
  Pallas kernels  78.5 us (97%)
  local copies, waits for them, and re-layouts  1.94 us (2%)
    pallas_call x1, Pallas kernels, local(): pl.pallas_call(kernel, out_shape=jax.ShapeDtypeStruct((ROWS, COLS), bf16)...  78.5 us
    unnamed x1, local copies, waits for them, and re-layouts  1.94 us

profile of v5, /device:TPU:1, one launch (start us, length us, event | category | flops | bytes accessed | tf_op | source)
XLA Modules:
  0.0 80.4 jit_solution(3428178194328490622)
XLA Ops:
  0.0 78.5 %shard_map.64 = bf16[768,384]{1,0:T(8,128)(2,1)} custom-call(s32[2,6]{1,0:T(2,128)} %tiles_ref.1, s32[2]{0:T(128)} %counts_ref.1, bf16[48,4096]{1,0:T(8,128)(2,1)} %q_hbm.1, bf16[48,4096]{1,0:T(8,128)(2,1)} %k_hbm.1, bf16[48,4096]{1,0:T(8,128)(2,1)} %v_hbm.1, bf16[128,384]{1,0:T(8,128)(2,1)} %w_hbm.1), custom_call_target="tpu_custom_call" | custom-call | tf_op jit(solution)/shard_map/pallas_call | solution.py:476
  78.5 1.9 %copy.8 = bf16[768,384]{1,0:T(8,128)(2,1)} copy(bf16[768,384]{1,0:T(8,128)(2,1)} %shard_map.64) | data formatting | bytes 1179648

commit v6 on v5

--- a/solution.py
+++ b/solution.py
@@ -421,14 +421,14 @@
     halo_start(1)
     meet_wait(2)
     meet_signal(3)
+    a2a_wait(2)
     w_local.wait()
     share(0).start()
-    a2a_wait(2)
+    far_start(False)
     meet_wait(3)
+    far_start(True)
     halo_wait_recv(0)
     halo_wait_recv(1)
-    far_start(False)
-    far_start(True)
     attention(0)
     attention(1)
     send_second(0)

time: 81.2 us -> 79.9 us (0.984)
  no operation moved by 1% of the time
where the time goes in v6:
time: 79.9 us; the launch traced here: 79.7 us
  Pallas kernels  77.7 us (97%)
  local copies, waits for them, and re-layouts  1.94 us (2%)
    pallas_call x1, Pallas kernels, local(): pl.pallas_call(kernel, out_shape=jax.ShapeDtypeStruct((ROWS, COLS), bf16)...  77.7 us
    unnamed x1, local copies, waits for them, and re-layouts  1.94 us

profile of v6, /device:TPU:1, one launch (start us, length us, event | category | flops | bytes accessed | tf_op | source)
XLA Modules:
  0.0 79.7 jit_solution(8747976120228943410)
XLA Ops:
  0.0 77.7 %shard_map.64 = bf16[768,384]{1,0:T(8,128)(2,1)} custom-call(s32[2,6]{1,0:T(2,128)} %tiles_ref.1, s32[2]{0:T(128)} %counts_ref.1, bf16[48,4096]{1,0:T(8,128)(2,1)} %q_hbm.1, bf16[48,4096]{1,0:T(8,128)(2,1)} %k_hbm.1, bf16[48,4096]{1,0:T(8,128)(2,1)} %v_hbm.1, bf16[128,384]{1,0:T(8,128)(2,1)} %w_hbm.1), custom_call_target="tpu_custom_call" | custom-call | tf_op jit(solution)/shard_map/pallas_call | solution.py:476
  77.7 1.9 %copy.8 = bf16[768,384]{1,0:T(8,128)(2,1)} copy(bf16[768,384]{1,0:T(8,128)(2,1)} %shard_map.64) | data formatting | bytes 1179648
